TPU v7x, 512 devices: a whole 4x8x8 slice. The times are simulated.
512 devices in a mesh: row: 32 (over x_lo, z, core), col: 16 (over y, x_hi).
Axes of the slice: x: 4 (x_hi: 2, x_lo: 2; x = x_hi * 2 + x_lo), y: 8, z: 8, core: 2. Of those that a mesh axis runs over, the one named last changes fastest.
Arguments:
- change: bfloat16 [16384, 53248], P('row', 'col'), may hold values from -50 to 50
- test_matrix: bfloat16 [53248, 128], P('col'), may hold values from -6 to 6
Outputs:
- scaled_left_basis: float32 [16384, 128], P(('row', 'col'))
- adapter_up_factor: float32 [16384, 128], P(('row', 'col'))
- adapter_down_factor: bfloat16 [53248, 128], P('col')
All inputs are finite; a program needn't handle non-finite values.
Results may differ from a plain program's by a relative error of at most 0.012.
Values may be sent and summed in bfloat16 or wider, within the bound.
No kernel may reach another device: no remote copies, remote signals or barrier semaphores. Data moves between devices by JAX's collectives and lax.ppermute only.
A program may use at most 64 MiB of HBM per device.

v0:
```python
import math

import jax
import jax.numpy as jnp
from jax import lax
from jax.sharding import PartitionSpec as P

WIDTH = 16384
HIDDEN_COLUMNS = 53248


def gram_of(tall):
    return lax.dot_general(
        tall,
        tall,
        (((0,), (0,)), ((), ())),
        precision=lax.Precision.HIGHEST,
        preferred_element_type=jnp.float32,
    )


def orthonormal(tall, gram_sum):
    lower_factor = jnp.linalg.cholesky(gram_sum)
    solved = jax.scipy.linalg.solve_triangular(lower_factor, tall.T, lower=True)
    return solved.T


def on_device(change, test_matrix):
    rows_dev = change.shape[0]
    share_rows = rows_dev // lax.axis_size("col")
    col_place = lax.axis_index("col")
    partial_sketch = jnp.dot(change, test_matrix, preferred_element_type=jnp.float32)
    sketch = lax.psum(partial_sketch, "col")
    left_gram = lax.psum(gram_of(sketch), "row")
    left_q32 = orthonormal(sketch, left_gram)
    left_q = left_q32.astype(jnp.bfloat16)
    own_left = lax.dynamic_slice_in_dim(left_q32, col_place * share_rows, share_rows, 0)
    scaled_left_basis = own_left * math.sqrt(WIDTH)
    partial_right = lax.dot_general(
        change, left_q, (((0,), (0,)), ((), ())), preferred_element_type=jnp.float32
    )
    transposed = lax.psum(partial_right, "row")
    right_gram = lax.psum(gram_of(transposed), "col")
    right_orthonormal = orthonormal(transposed, right_gram).astype(jnp.bfloat16)
    adapter_down_factor = (
        right_orthonormal.astype(jnp.float32) * math.sqrt(HIDDEN_COLUMNS)
    ).astype(jnp.bfloat16)
    adapter_up_factor = lax.psum_scatter(
        jnp.dot(change, right_orthonormal, preferred_element_type=jnp.float32),
        "col",
        scatter_dimension=0,
        tiled=True,
    )
    return (scaled_left_basis, adapter_up_factor, adapter_down_factor)


def solution(mesh):
    in_specs = (P("row", "col"), P("col", None))
    out_specs = (P(("row", "col"), None), P(("row", "col"), None), P("col", None))
    return jax.shard_map(
        on_device, mesh=mesh, in_specs=in_specs, out_specs=out_specs, check_vma=False
    )
```

profile of v0, /device:TPU:1, one launch (start us, length us, event | category | flops | bytes accessed | tf_op | source)
XLA Modules:
  0.0 1032.7 jit_solution(8475018877697604453)
XLA Ops:
  7.2 1.9 copy-done
  9.1 2.9 fusion.8
  12.1 0.0 all-reduce.7.cloned.1.call-start
  12.1 157.5 %all-reduce.5.cloned.1.call-done = f32[512,128]{1,0:T(8,128)} async-done(((f32[512,128]{1,0:T(8,128)}), f32[512,128]{1,0:T(8,128)}) %all-reduce.5.cloned.1.call-update) | async-done | bytes 262160 | tf_op jit(solution)/shard_map/psum | solution.py:33
  169.6 2.2 fusion.9
  171.9 0.0 all-reduce.9.cloned.1.call-start
  171.9 206.3 %all-reduce.7.cloned.1.call-done = f32[128,128]{0,1:T(8,128)} async-done(((f32[128,128]{0,1:T(8,128)}), f32[128,128]{0,1:T(8,128)}) %all-reduce.7.cloned.1.call-update) | async-done | bytes 65552 | tf_op jit(solution)/shard_map/psum | solution.py:34
  378.3 0.9 copy.11
  379.2 0.9 fusion.7
  380.1 11.7 %cholesky.44 = f32[128,128]{1,0:T(8,128)S(1)} custom-call(f32[128,128]{1,0:T(8,128)S(1)} %fusion.7), custom_call_target="Cholesky" | custom-call | tf_op jit(solution)/shard_map/jit(cholesky)/cholesky | solution.py:23
  391.8 0.6 compare_reduce_fusion.1
  392.5 0.7 fusion.1
  393.1 9.8 custom-call.10
  402.9 1.3 fusion.5
  404.3 0.7 copy-done.1
  405.0 1.8 convolution_bitcast_fusion
  406.8 0.0 all-reduce.11.cloned.1.call-start
  406.9 229.8 %all-reduce.9.cloned.1.call-done = f32[3328,128]{0,1:T(8,128)} async-done(((f32[3328,128]{0,1:T(8,128)}), f32[3328,128]{0,1:T(8,128)}) %all-reduce.9.cloned.1.call-update) | async-done | bytes 1703952 | tf_op jit(solution)/shard_map/psum | solution.py:42
  636.7 4.1 fusion.10
  640.8 0.2 reduce-scatter.4.cloned.1.call-start
  641.1 144.5 %all-reduce.11.cloned.1.call-done = f32[128,128]{0,1:T(8,128)} async-done(((f32[128,128]{0,1:T(8,128)}), f32[128,128]{0,1:T(8,128)}) %all-reduce.11.cloned.1.call-update) | async-done | bytes 65552 | tf_op jit(solution)/shard_map/psum | solution.py:43
  785.6 0.9 copy.13
  786.5 0.9 fusion.4
  787.3 11.7 %cholesky.55 = f32[128,128]{1,0:T(8,128)S(1)} custom-call(f32[128,128]{1,0:T(8,128)S(1)} %fusion.4), custom_call_target="Cholesky" | custom-call | tf_op jit(solution)/shard_map/jit(cholesky)/cholesky | solution.py:23
  799.1 0.6 compare_reduce_fusion
  799.7 0.7 fusion.2
  800.4 9.8 custom-call.11
  810.2 5.2 multiply_convert_fusion
  815.4 2.0 convolution_bitcast_fusion.1
  817.4 1.8 copy.17
  819.2 1.3 dynamic-slice_multiply_fusion
  820.5 205.7 %reduce-scatter.4.cloned.1.call-done = f32[32,128]{1,0:T(8,128)} async-done(((f32[512,128]{1,0:T(8,128)}), f32[32,128]{1,0:T(8,128)}) %reduce-scatter.4.cloned.1.call-update) | async-done | bytes 16400
  (10 shorter events, 0.2 us)
Async XLA Ops:
  7.2 2.0 copy-start
  7.2 162.4 %all-reduce.5.cloned.1.call-start = ((), (), s32[]{:S(2)}) async-start(), calls=%async_computation.1 | async-start | bytes 524288 | tf_op jit(solution)/shard_map/psum | solution.py:33
  12.1 366.2 %all-reduce.7.cloned.1.call-start = ((), (), s32[]{:S(2)}) async-start(), calls=%async_computation.2 | async-start | bytes 131072 | tf_op jit(solution)/shard_map/psum | solution.py:34
  171.9 464.8 %all-reduce.9.cloned.1.call-start = ((), (), s32[]{:S(2)}) async-start(), calls=%async_computation.3 | async-start | bytes 3407872 | tf_op jit(solution)/shard_map/psum | solution.py:42
  404.2 0.7 copy-start.1
  406.8 378.7 %all-reduce.11.cloned.1.call-start = ((), (), s32[]{:S(2)}) async-start(), calls=%async_computation.4 | async-start | bytes 131072 | tf_op jit(solution)/shard_map/psum | solution.py:43
  640.8 385.4 %reduce-scatter.4.cloned.1.call-start = ((), (), s32[]{:S(2)}) async-start(), calls=%async_computation.5 | async-start | bytes 278528
Sparse Core Ops, SparseCore 0:
  12.2 157.3 all-reduce.4
  173.4 204.8 all-reduce.6
  406.9 229.7 all-reduce.8
  641.0 144.5 all-reduce.10
  819.3 206.8 reduce-scatter.3
where the time goes:
time: 1040 us; the launch traced here: 1030 us
  waiting for transfers between devices  944 us (91%)
  other arithmetic  48.7 us (5%)
  matrix products  19.6 us (2%)
  between operations  13.9 us (1%)
    psum x1, waiting for transfers between devices, on_device(): transposed = lax.psum(partial_right, 'row')  230 us
    psum x1, waiting for transfers between devices, on_device(): left_gram = lax.psum(gram_of(sketch), 'row')  206 us
    unnamed x6, waiting for transfers between devices  206 us
    psum x1, waiting for transfers between devices, on_device(): sketch = lax.psum(partial_sketch, 'col')  158 us
    psum x1, waiting for transfers between devices, on_device(): right_gram = lax.psum(gram_of(transposed), 'col')  144 us
    another operation x6, other arithmetic, orthonormal(): lower_factor = jnp.linalg.cholesky(gram_sum)  24.8 us
    another operation x4, other arithmetic, orthonormal(): solved = jax.scipy.linalg.solve_triangular(lower_factor, tall.T, lower=True)  20.9 us
  transfers between devices with their start and end apart: 5, of which 5 were waited for; matrix products, arithmetic and copies ran while one was open for 0% of the time, Pallas kernels for 0%

commit v1 on v0

v1 whole, which is shorter than its diff:
```python
import math

import jax
import jax.numpy as jnp
from jax import lax
from jax.experimental import pallas as pl
from jax.experimental.pallas import tpu as pltpu
from jax.sharding import PartitionSpec as P

WIDTH = 16384
HIDDEN_COLUMNS = 53248
SKETCH = 128
SUB = 8
BF16 = jnp.bfloat16
F32 = jnp.float32


def inverse_factor(gram):
    blocks = [gram[SUB * b : SUB * (b + 1), :] for b in range(SKETCH // SUB)]
    lane = lax.broadcasted_iota(jnp.int32, (SUB, SKETCH), 1)
    sub = lax.broadcasted_iota(jnp.int32, (SUB, SKETCH), 0)
    for j in range(SKETCH):
        b, s = divmod(j, SUB)
        row = blocks[b][s : s + 1, :]
        scaled = jnp.where(lane[:1] == j, 1.0, row) * (1.0 / row[:, j : j + 1])
        for i in range(b, SKETCH // SUB):
            if i == b and s == SUB - 1:
                continue
            below = jnp.where(lane == j, 0.0, blocks[i]) - blocks[i][:, j : j + 1] * scaled
            blocks[i] = jnp.where(sub > s, below, blocks[i]) if i == b else below
    rows = []
    for b, block in enumerate(blocks):
        on_diagonal = lane == sub + SUB * b
        pivot = jnp.sum(jnp.where(on_diagonal, block, 0.0), axis=1, keepdims=True)
        root = lax.rsqrt(pivot)
        root = root * (1.5 - 0.5 * pivot * root * root)
        rows.append(jnp.where(on_diagonal, root, jnp.where(lane < sub + SUB * b, block * root, 0.0)))
    return jnp.concatenate(rows, axis=0)


def factor_kernel(gram_ref, inverse_ref):
    inverse_ref[...] = inverse_factor(gram_ref[...])


def inverse_cholesky(gram):
    return pl.pallas_call(factor_kernel, out_shape=jax.ShapeDtypeStruct(gram.shape, F32))(gram)


def split(value):
    high = value.astype(BF16)
    return high, (value - high.astype(F32)).astype(BF16)


def times_transposed(tall, square, precision=None):
    return lax.dot_general(
        tall, square, (((1,), (1,)), ((), ())), precision=precision, preferred_element_type=F32
    )


def gram_of(tall):
    return lax.dot_general(tall, tall, (((0,), (0,)), ((), ())), preferred_element_type=F32)


def spread(value, copies):
    return jnp.broadcast_to(value[None], (copies, *value.shape))


def on_device(change, test_matrix):
    rows_dev, cols_dev = change.shape
    n_col, n_row = lax.axis_size("col"), lax.axis_size("row")
    half = n_row // 2
    share = rows_dev // n_col
    part = cols_dev // n_row
    gram_part = SKETCH // n_row
    pairs = [[2 * i, 2 * i + 1] for i in range(half)]
    same_core = [[2 * i + c for i in range(half)] for c in range(2)]

    def swap(value, axis, groups=None):
        return lax.all_to_all(value, axis, 0, 0, axis_index_groups=groups, tiled=True)

    partial = jnp.dot(change, test_matrix, preferred_element_type=F32).astype(BF16)
    pieces = swap(partial.reshape(n_col, share, SKETCH), "col")
    own_sketch = pieces.astype(F32).sum(0).astype(BF16)
    sketch = swap(spread(own_sketch, n_col), "col").reshape(rows_dev, SKETCH)

    def pack(tall, gram):
        return jnp.concatenate([tall.astype(BF16), *split(gram)], axis=-2)

    def total(packed):
        packed = packed.astype(F32).sum(0)
        tall, high, low = jnp.split(packed, (part, part + gram_part), axis=-2)
        return tall, high + low

    raw = lax.dot_general(change, sketch, (((0,), (0,)), ((), ())), preferred_element_type=F32)
    packed = pack(
        raw.reshape(2, half, part, SKETCH), gram_of(sketch).reshape(2, half, gram_part, SKETCH)
    )
    packed = pack(*total(swap(packed, "row", pairs)))
    packed = pack(*total(swap(packed, "row", same_core)))
    packed = swap(spread(packed, half), "row", same_core)
    packed = swap(spread(packed, 2), "row", pairs)
    packed = packed.reshape(n_row, part + 2 * gram_part, SKETCH)
    raw = packed[:, :part].reshape(cols_dev, SKETCH)
    left_gram = packed[:, part : part + gram_part].astype(F32) + packed[:, part + gram_part :].astype(F32)
    left_inverse = inverse_cholesky(left_gram.reshape(SKETCH, SKETCH))
    scaled_left_basis = math.sqrt(WIDTH) * times_transposed(
        own_sketch.astype(F32), left_inverse, lax.Precision.HIGHEST
    )
    high, low = split(left_inverse)
    transposed = (times_transposed(raw, high) + times_transposed(raw, low)).astype(BF16)

    core = lax.axis_index("row") % 2
    partial = jnp.dot(change, transposed, preferred_element_type=F32).reshape(n_col, share, SKETCH)
    gram_half = lax.dynamic_slice_in_dim(gram_of(transposed), core * (SKETCH // 2), SKETCH // 2, 0)
    packed = jnp.concatenate([partial, spread(gram_half, n_col)], axis=1)
    packed = swap(packed, "col").sum(0)
    right_gram = swap(spread(packed[share:], 2), "row", pairs).reshape(SKETCH, SKETCH)
    right_inverse = inverse_cholesky(right_gram)
    high, low = split(right_inverse)
    right = (times_transposed(transposed, high) + times_transposed(transposed, low)).astype(BF16)
    adapter_down_factor = (right.astype(F32) * math.sqrt(HIDDEN_COLUMNS)).astype(BF16)
    adapter_up_factor = times_transposed(packed[:share], right_inverse, lax.Precision.HIGHEST)
    return (scaled_left_basis, adapter_up_factor, adapter_down_factor)


def solution(mesh):
    in_specs = (P("row", "col"), P("col", None))
    out_specs = (P(("row", "col"), None), P(("row", "col"), None), P("col", None))
    return jax.shard_map(
        on_device, mesh=mesh, in_specs=in_specs, out_specs=out_specs, check_vma=False
    )
```

time: 1040 us -> 180 us (0.17)
  waiting for transfers between devices: 944 us -> 33.5 us
  blocking collectives: 0 us -> 76.7 us
  other arithmetic: 48.7 us -> 5.3 us
  Pallas kernels: 0 us -> 24.6 us
  between operations: 13.9 us -> 0.84 us
    psum x4 -> x0, waiting for transfers between devices: 738 us -> none  [the longest x1 230 us: on_device(): transposed = lax.psum(partial_right, 'row')]
    unnamed x6 -> x0, waiting for transfers between devices: 206 us -> none
    all_to_all x0 -> x6, blocking collectives: none -> 76.7 us  [swap(): lax.all_to_all(value, axis, 0, 0, axis_index_groups=groups, tiled=True)]
    another operation x10 -> x0, other arithmetic: 45.7 us -> none  [the longest x6 24.8 us: orthonormal(): lower_factor = jnp.linalg.cholesky(gram_sum)]
    all_to_all x0 -> x2, waiting for transfers between devices: none -> 33.5 us  [swap(): lax.all_to_all(value, axis, 0, 0, axis_index_groups=groups, tiled=True)]
    pallas_call x0 -> x2, Pallas kernels: none -> 24.6 us  [inverse_cholesky(): pl.pallas_call(factor_kernel, out_shape=jax.ShapeDtypeStruct(gram.shape,...]
    all_to_all x0 -> x2, starting transfers between devices: none -> 10.7 us  [swap(): lax.all_to_all(value, axis, 0, 0, axis_index_groups=groups, tiled=True)]
  transfers between devices with their start and end apart: 5 -> 2, of which waited for: 5 -> 2; matrix products, arithmetic and copies ran while one was open for 0% -> 0% of each run, Pallas kernels for 0% -> 0%
where the time goes in v1:
time: 180 us; the launch traced here: 179 us
  blocking collectives  76.7 us (43%)
  waiting for transfers between devices  33.5 us (19%)
  Pallas kernels  24.6 us (14%)
  matrix products  14.6 us (8%)
  local copies, waits for them, and re-layouts  13.1 us (7%)
  starting transfers between devices  10.7 us (6%)
  other arithmetic  5.3 us (3%)
    all_to_all x6, blocking collectives, swap(): lax.all_to_all(value, axis, 0, 0, axis_index_groups=groups, tiled=True)  76.7 us
    all_to_all x2, waiting for transfers between devices, swap(): lax.all_to_all(value, axis, 0, 0, axis_index_groups=groups, tiled=True)  33.5 us
    pallas_call x2, Pallas kernels, inverse_cholesky(): pl.pallas_call(factor_kernel, out_shape=jax.ShapeDtypeStruct(gram.shape,...  24.6 us
    all_to_all x2, starting transfers between devices, swap(): lax.all_to_all(value, axis, 0, 0, axis_index_groups=groups, tiled=True)  10.7 us
    dot_general x6, matrix products, times_transposed(): lax.dot_general(tall, square, (((1,), (1,)), ((), ())), precision=precisi...  7.38 us
  transfers between devices with their start and end apart: 2, of which 2 were waited for; matrix products, arithmetic and copies ran while one was open for 0% of the time, Pallas kernels for 0%

profile of v1, /device:TPU:1, one launch (start us, length us, event | category | flops | bytes accessed | tf_op | source)
XLA Modules:
  0.0 179.3 jit_solution(11403539545443736633)
XLA Ops:
  0.6 2.0 %copy-done = bf16[512,3328]{1,0:T(8,128)(2,1)S(1)} copy-done((bf16[512,3328]{1,0:T(8,128)(2,1)S(1)}, bf16[512,3328]{1,0:T(8,128)(2,1)}, u32[]{:S(2)}) %copy-start) | copy-done | bytes 3407896
  2.6 2.2 %convolution_convert_fusion.1 = bf16[512,128]{1,0:T(8,128)(2,1)S(1)} fusion(bf16[512,3328]{1,0:T(8,128)(2,1)S(1)} %copy-done, bf16[3328,128]{1,0:T(8,128)(2,1)} %param.3), kind=kOutput, calls=%fused_computation.11 | convolution fusion | flops 436273152 | bytes 4390912 | tf_op jit(solution)/shard_map/dot_general | solution.py:81
  4.8 20.0 %all_to_all.40 = bf16[16,32,128]{2,1,0:T(8,128)(2,1)S(1)} all-to-all(bf16[16,32,128]{2,1,0:T(8,128)(2,1)S(1)} %bitcast.45), channel_id=1, replica_groups=mesh['row'=32,'col'=16] {'col'}, dimensions={0} | all-to-all | bytes 262144 | tf_op jit(solution)/shard_map/all_to_all | solution.py:79
  24.8 12.6 %all_to_all.41 = bf16[16,32,128]{2,1,0:T(8,128)(2,1)S(1)} all-to-all(bf16[16,32,128]{2,1,0:T(8,128)(2,1)S(1)} %broadcast_in_dim.10), channel_id=1, replica_groups=mesh['row'=32,'col'=16] {'col'}, dimensions={0} | all-to-all | bytes 262144 | tf_op jit(solution)/shard_map/all_to_all | solution.py:79
  37.5 0.8 copy.16
  38.3 1.6 dot_general.42
  39.8 1.1 subtract_convert_fusion.2
  42.1 1.6 fusion.5
  43.7 2.2 %copy.15 = bf16[3328,128]{1,0:T(8,128)(2,1)} copy(bf16[3328,128]{0,1:T(8,128)(2,1)} %fusion.5) | data formatting | bytes 1703936 | tf_op jit(solution)/shard_map/convert_element_type | solution.py:87
  45.9 1.3 pad_maximum_fusion
  47.2 7.3 %all_to_all.42 = bf16[2,16,112,128]{3,2,1,0:T(8,128)(2,1)S(1)} all-to-all(bf16[2,16,112,128]{3,2,1,0:T(8,128)(2,1)S(1)} %pad_maximum_fusion), channel_id=1, replica_groups={{0,16},{32,48},{64,80},{96,112},{128,144},{160,176},{192,208},{224,240}..., dimensions={0} | all-to-all | bytes 1835008 | tf_op jit(solution)/shard_map/all_to_all | solution.py:79
  54.8 22.1 %all_to_all.43 = bf16[16,112,128]{2,1,0:T(8,128)(2,1)S(1)} all-to-all(bf16[16,112,128]{2,1,0:T(8,128)(2,1)S(1)} %pad_maximum_fusion.2), channel_id=1, replica_groups={{0,32,64,96,128,160,192,224,256,288,320,352,384,416,448,480},{16,48,80,..., dimensions={0} | all-to-all | bytes 917504 | tf_op jit(solution)/shard_map/all_to_all | solution.py:79
  77.0 0.8 broadcast_in_dim.11
  77.8 6.5 %all-to-all-start.4 = ((bf16[16,112,128]{2,1,0:T(8,128)(2,1)}), bf16[16,112,128]{2,1,0:T(8,128)(2,1)}, u32[]{:S(2)}, u32[]{:S(2)}) async-start(bf16[16,112,128]{2,1,0:T(8,128)(2,1)} %broadcast_in_dim.11), calls=%async_computation.4 | async-start | bytes 917504 | tf_op jit(solution)/shard_map/all_to_all | solution.py:79
  84.3 11.9 %all-to-all-done.4 = bf16[16,112,128]{2,1,0:T(8,128)(2,1)} async-done(((bf16[16,112,128]{2,1,0:T(8,128)(2,1)}), bf16[16,112,128]{2,1,0:T(8,128)(2,1)}, u32[]{:S(2)}, u32[]{:S(2)}) %all-to-all-start.4) | async-done | bytes 458784 | tf_op jit(solution)/shard_map/all_to_all | solution.py:79
  96.3 1.1 broadcast_in_dim.12
  97.4 7.0 %all_to_all.44 = bf16[2,16,112,128]{3,2,1,0:T(8,128)(2,1)S(1)} all-to-all(bf16[2,16,112,128]{3,2,1,0:T(8,128)(2,1)S(1)} %broadcast_in_dim.12), channel_id=1, replica_groups={{0,16},{32,48},{64,80},{96,112},{128,144},{160,176},{192,208},{224,240}..., dimensions={0} | all-to-all | bytes 1835008 | tf_op jit(solution)/shard_map/all_to_all | solution.py:79
  105.1 1.0 slice.22
  106.0 12.3 %shard_map.49 = f32[128,128]{1,0:T(8,128)} custom-call(f32[128,128]{1,0:T(8,128)} %bitcast.43), custom_call_target="tpu_custom_call" | custom-call | tf_op jit(solution)/shard_map/pallas_call | solution.py:46
  118.3 1.6 fusion.14
  121.3 2.0 %convolution_bitcast_fusion = f32[512,128]{0,1:T(8,128)} fusion(bf16[3328,128]{1,0:T(8,128)(2,1)S(1)} %fusion, bf16[512,3328]{1,0:T(8,128)(2,1)S(1)} %copy-done), kind=kOutput, calls=%fused_computation.10 | convolution fusion | flops 436207616 | bytes 4521984 | tf_op jit(solution)/shard_map/dot_general | solution.py:113
  123.2 1.8 copy.20
  125.0 1.9 %pad_maximum_fusion.1 = f32[16,96,128]{2,1,0:T(8,128)} fusion(f32[16,64,128]{2,1,0:T(8,128)S(1)} %broadcast_in_dim.13, f32[16,32,128]{2,1,0:T(8,128)} %bitcast.42), kind=kLoop, calls=%fused_computation.16 | loop fusion | flops 196608 | bytes 1572864 | tf_op jit(solution)/shard_map/concatenate | solution.py:115
  126.9 4.3 %all-to-all-start.6 = ((f32[16,96,128]{2,1,0:T(8,128)}), f32[16,96,128]{2,1,0:T(8,128)}, u32[]{:S(2)}, u32[]{:S(2)}) async-start(f32[16,96,128]{2,1,0:T(8,128)} %pad_maximum_fusion.1), calls=%async_computation.6 | async-start | bytes 1572864 | tf_op jit(solution)/shard_map/all_to_all | solution.py:79
  131.2 0.8 convolution_multiply_fusion
  132.0 21.6 %all-to-all-done.6 = f32[16,96,128]{2,1,0:T(8,128)} async-done(((f32[16,96,128]{2,1,0:T(8,128)}), f32[16,96,128]{2,1,0:T(8,128)}, u32[]{:S(2)}, u32[]{:S(2)}) %all-to-all-start.6) | async-done | bytes 786464 | tf_op jit(solution)/shard_map/all_to_all | solution.py:79
  153.6 1.2 reduce_sum.42
  154.8 7.6 %all_to_all.45 = f32[2,64,128]{2,1,0:T(8,128)} all-to-all(f32[2,64,128]{2,1,0:T(8,128)S(1)} %broadcast_in_dim.14), channel_id=1, replica_groups={{0,16},{32,48},{64,80},{96,112},{128,144},{160,176},{192,208},{224,240}..., dimensions={0} | all-to-all | bytes 131072 | tf_op jit(solution)/shard_map/all_to_all | solution.py:79
  162.4 12.3 %shard_map.50 = f32[128,128]{1,0:T(8,128)} custom-call(f32[128,128]{1,0:T(8,128)} %bitcast.44), custom_call_target="tpu_custom_call" | custom-call | tf_op jit(solution)/shard_map/pallas_call | solution.py:46
  174.7 1.7 fusion.8
  176.5 1.5 fusion.11
  178.0 1.3 fusion.4
  (30 shorter events, 3.6 us)
Async XLA Ops:
  0.6 2.0 %copy-start = (bf16[512,3328]{1,0:T(8,128)(2,1)S(1)}, bf16[512,3328]{1,0:T(8,128)(2,1)}, u32[]{:S(2)}) copy-start(bf16[512,3328]{1,0:T(8,128)(2,1)} %param.2) | copy-start | bytes 10223620
  77.8 18.4 %all-to-all-start.4 = ((bf16[16,112,128]{2,1,0:T(8,128)(2,1)}), bf16[16,112,128]{2,1,0:T(8,128)(2,1)}, u32[]{:S(2)}, u32[]{:S(2)}) async-start(bf16[16,112,128]{2,1,0:T(8,128)(2,1)} %broadcast_in_dim.11), calls=%async_computation.4 | async-start | bytes 917504 | tf_op jit(solution)/shard_map/all_to_all | solution.py:79
  118.3 1.6 copy-start.3
  118.3 1.6 copy-start.4
  120.3 0.9 copy-start.1
  126.9 26.7 %all-to-all-start.6 = ((f32[16,96,128]{2,1,0:T(8,128)}), f32[16,96,128]{2,1,0:T(8,128)}, u32[]{:S(2)}, u32[]{:S(2)}) async-start(f32[16,96,128]{2,1,0:T(8,128)} %pad_maximum_fusion.1), calls=%async_computation.6 | async-start | bytes 1572864 | tf_op jit(solution)/shard_map/all_to_all | solution.py:79
  174.7 3.3 %copy-start.2 = (bf16[3328,128]{1,0:T(8,128)(2,1)S(1)}, bf16[3328,128]{1,0:T(8,128)(2,1)}, u32[]{:S(2)}) copy-start(bf16[3328,128]{1,0:T(8,128)(2,1)} %copy-done.1) | copy-start | bytes 2555908
  174.7 3.3 %copy-start.5 = (f32[128,128]{1,0:T(8,128)S(1)}, f32[128,128]{1,0:T(8,128)}, u32[]{:S(2)}) copy-start(f32[128,128]{1,0:T(8,128)} %shard_map.50) | copy-start | bytes 196612
